TPU v7x, 256 devices: a whole 4x4x8 slice. The times are simulated.
256 devices in a mesh: dom: 256 (over x, y, z, core).
Axes of the slice: x: 4, y: 4, z: 8, core: 2. Of those that a mesh axis runs over, the one named last changes fastest.
Arguments:
- x_block: float32 [8, 393216], P(None, 'dom'), may hold values from -18 to 18
- p_block: float32 [8, 393216], P(None, 'dom'), may hold values from -18 to 18
- stiff_elem: float32 [20, 20, 65536], P(None, None, 'dom'), may hold values from -6 to 12.4, as said below
- mass_elem: float32 [20, 20, 65536], P(None, None, 'dom'), may hold values from -0.03 to 0.7, as said below
- node_elem: float32 [10, 10, 65536], P(None, None, 'dom'), may hold values from -1 to 6.1, as said below
- elem_edge: int32 [20, 65536], P(None, 'dom'), may hold values from 0 to 1919, as said below
- elem_node: int32 [10, 65536], P(None, 'dom'), may hold values from 0 to 575, as said below
- send_edge: int32 [6, 16384], P(None, 'dom'), may hold values from 0 to 1535, as said below
- send_node: int32 [6, 8192], P(None, 'dom'), may hold values from 0 to 383, as said below
- grad_pairs: int32 [2, 393216], P(None, 'dom'), may hold values from 0 to 575, as said below
Outputs:
- w_block: float32 [8, 393216], P(None, 'dom')
- gram_stiff: float32 [24, 24], replicated
- gram_mass: float32 [24, 24], replicated
Inputs may be any that keep to these rules, and one draw needn't show every extreme that they name: `stiff_elem`: each element's matrix is symmetric and positive definite. `mass_elem`: each element's matrix is symmetric and positive definite. `node_elem`: each element's matrix is symmetric and positive definite. `elem_edge`: the 20 entries of one element are distinct, and every entry of a subdomain's extended edge list is used by some element of that subdomain. `elem_node`: the 10 entries of one element are distinct, and every entry of a subdomain's extended nodal list is used by some element of that subdomain. `send_edge`: the 64 entries of one direction of one subdomain are distinct. `send_node`: the 32 entries of one direction of one subdomain are distinct. `grad_pairs`: the tail and head of one edge unknown differ.
All inputs are finite; a program needn't handle non-finite values.
Results may differ from a plain program's by a relative error of at most 0.0001.
Values sent between devices are 32-bit elements; how exact they have to be, the bound alone decides.
A program may use at most 128 MiB of HBM per device.

v0:
```python
import jax
import jax.numpy as jnp
from jax import lax
from jax.sharding import PartitionSpec as P

CHEB_DEG = 3
NNODE = 384
highest = lax.Precision.HIGHEST
OFFSETS = (1, -1, 4, -4, 16, -16)
interval_low = 0.3
interval_high = 1.7
jacobi_weight = 0.7


def from_behind(shard, axis, by):
    length = lax.axis_size(axis)
    return lax.ppermute(shard, axis, [(i, (i + by) % length) for i in range(length)])


def edge_extend(values, send_edge):
    pieces = [values]
    for direction in range(6):
        outgoing = values[:, send_edge[direction]]
        pieces.append(from_behind(outgoing, "dom", OFFSETS[direction]))
    return jnp.concatenate(pieces, axis=1)


def edge_return(extended, send_edge):
    ghosts = send_edge.shape[1]
    owned = extended.shape[1] - 6 * ghosts
    total = extended[:, :owned]
    for direction in range(6):
        start = owned + direction * ghosts
        back = from_behind(extended[:, start : start + ghosts], "dom", -OFFSETS[direction])
        total = total.at[:, send_edge[direction]].add(back)
    return total


def node_extend(values, send_node):
    pieces = [values]
    for direction in range(6):
        outgoing = values[:, send_node[direction]]
        pieces.append(from_behind(outgoing, "dom", OFFSETS[direction]))
    return jnp.concatenate(pieces, axis=1)


def node_return(extended, send_node):
    ghosts = send_node.shape[1]
    owned = extended.shape[1] - 6 * ghosts
    total = extended[:, :owned]
    for direction in range(6):
        start = owned + direction * ghosts
        back = from_behind(extended[:, start : start + ghosts], "dom", -OFFSETS[direction])
        total = total.at[:, send_node[direction]].add(back)
    return total


def element_terms(matrices, values):
    return jnp.einsum("jke,cke->cje", matrices, values, precision=highest)


def scatter_local(terms, connect, length):
    return jnp.zeros((terms.shape[0], length), jnp.float32).at[:, connect].add(terms)


def inner_rows(left, right):
    return jnp.einsum("cn,dn->cd", left, right, precision=highest)


def arrange(pair_part, row_part, modes):
    mode_mode = pair_part[:, :modes, :modes]
    mode_prev = pair_part[:, :modes, modes:]
    prev_mode = pair_part[:, modes:, :modes]
    prev_prev = pair_part[:, modes:, modes:]
    new_mode = jnp.swapaxes(row_part[:, :, :modes], 1, 2)
    new_prev = jnp.swapaxes(row_part[:, :, 2 * modes :], 1, 2)
    upper = jnp.concatenate([mode_mode, new_mode, mode_prev], axis=2)
    lower = jnp.concatenate([prev_mode, new_prev, prev_prev], axis=2)
    return jnp.concatenate([upper, row_part, lower], axis=1)


def shards(
    x_block,
    p_block,
    stiff_elem,
    mass_elem,
    node_elem,
    elem_edge,
    elem_node,
    send_edge,
    send_node,
    grad_pairs,
):
    modes = x_block.shape[0]
    owned_edges = x_block.shape[1]
    edge_length = owned_edges + 6 * send_edge.shape[1]
    node_length = NNODE + 6 * send_node.shape[1]
    pair = jnp.concatenate([x_block, p_block], axis=0)
    pair_values = edge_extend(pair, send_edge)[:, elem_edge]
    stiff_pair = element_terms(stiff_elem, pair_values)
    mass_pair = element_terms(mass_elem, pair_values)
    edge_diag = edge_return(
        scatter_local(jnp.einsum("jje->je", stiff_elem)[None], elem_edge, edge_length), send_edge
    )[0]
    node_diag = node_return(
        scatter_local(jnp.einsum("jje->je", node_elem)[None], elem_node, node_length), send_node
    )[0]
    images = edge_return(
        scatter_local(jnp.concatenate([stiff_pair, mass_pair], axis=0), elem_edge, edge_length),
        send_edge,
    )
    stiff_x = images[:modes]
    stiff_p = images[modes : 2 * modes]
    mass_x = images[2 * modes : 3 * modes]
    mass_p = images[3 * modes :]
    numerator, denominator = lax.psum(
        (jnp.sum(x_block * stiff_x, axis=1), jnp.sum(x_block * mass_x, axis=1)), "dom"
    )
    quotient = numerator / denominator
    residual = stiff_x - quotient[:, None] * mass_x

    def stiff_image(vectors):
        values = edge_extend(vectors, send_edge)[:, elem_edge]
        return edge_return(
            scatter_local(element_terms(stiff_elem, values), elem_edge, edge_length), send_edge
        )

    center = 0.5 * (interval_high + interval_low)
    spread = 0.5 * (interval_high - interval_low)
    sigma = center / spread
    rho_now = 1.0 / sigma
    step_dir = residual / (center * edge_diag)
    smooth = step_dir
    for turn in range(CHEB_DEG - 1):
        rho_next = 1.0 / (2.0 * sigma - rho_now)
        remain = residual - stiff_image(smooth)
        step_dir = rho_next * rho_now * step_dir + 2.0 * rho_next / spread * remain / edge_diag
        smooth = smooth + step_dir
        rho_now = rho_next
    after = residual - stiff_image(smooth)
    tails = grad_pairs[0]
    heads = grad_pairs[1]
    gathered_res = (
        jnp.zeros((modes, node_length), jnp.float32)
        .at[:, heads]
        .add(after)
        .at[:, tails]
        .add(-after)
    )
    nodal_res = node_return(gathered_res, send_node)
    first = jacobi_weight * nodal_res / node_diag
    first_values = node_extend(first, send_node)[:, elem_node]
    node_image = node_return(
        scatter_local(element_terms(node_elem, first_values), elem_node, node_length), send_node
    )
    second = first + jacobi_weight * (nodal_res - node_image) / node_diag
    second_full = node_extend(second, send_node)
    w_block = smooth + second_full[:, heads] - second_full[:, tails]
    basis = jnp.concatenate([x_block, w_block, p_block], axis=0)
    w_values = edge_extend(w_block, send_edge)[:, elem_edge]
    stiff_wterm = element_terms(stiff_elem, w_values)
    mass_wterm = element_terms(mass_elem, w_values)
    w_images = edge_return(
        scatter_local(jnp.concatenate([stiff_wterm, mass_wterm], axis=0), elem_edge, edge_length),
        send_edge,
    )
    w_rows = jnp.stack([inner_rows(w_images[:modes], basis), inner_rows(w_images[modes:], basis)])
    stiff_part = inner_rows(pair, jnp.concatenate([stiff_x, stiff_p], axis=0))
    mass_part = inner_rows(pair, jnp.concatenate([mass_x, mass_p], axis=0))
    full_gram = lax.psum(arrange(jnp.stack([stiff_part, mass_part]), w_rows, modes), "dom")
    total_edges = owned_edges * lax.axis_size("dom")
    return (w_block, full_gram[0] / total_edges, full_gram[1] / total_edges)


def solution(mesh):
    in_specs = (
        P(None, "dom"),
        P(None, "dom"),
        P(None, None, "dom"),
        P(None, None, "dom"),
        P(None, None, "dom"),
        P(None, "dom"),
        P(None, "dom"),
        P(None, "dom"),
        P(None, "dom"),
        P(None, "dom"),
    )
    out_specs = (P(None, "dom"), P(), P())
    return jax.shard_map(shards, mesh=mesh, in_specs=in_specs, out_specs=out_specs, check_vma=False)
```

profile of v0, /device:TPU:1, one launch (start us, length us, event | category | flops | bytes accessed | tf_op | source)
XLA Modules:
  0.0 1168.0 jit_solution(15326669690173513750)
XLA Ops:
  13.2 6.9 collective-permute-start.3
  22.1 27.5 %scatter_custom_fusion.7 = f32[1920]{0:T(1024)S(1)} fusion(s32[5120]{0:T(1024)S(1)} %reshape.805, f32[5120]{0:T(1024)S(1)} %reshape.865, f32[]{:T(128)} %constant.12.clone.1), kind=kCustom, calls=%fused_computation.356 | custom fusion | flops 5120 | bytes 7684 | tf_op jit(solution)/shard_map/scatter-add | solution.py:63
  63.1 7.5 collective-permute-start.12
  76.2 18.8 %gather_fusion.6 = f32[5120,16]{1,0:T(8,128)} fusion(f32[16,1920]{0,1:T(8,128)} %constant_dynamic-update-slice_fusion.2, s32[5120]{0:T(1024)S(1)} %broadcast_clamp_fusion), kind=kCustom, calls=%fused_computation.6 | custom fusion | bytes 675840 | tf_op jit(solution)/shard_map/gather | solution.py:99
  98.9 7.3 fusion.7
  108.8 8.9 fusion.4
  125.9 29.0 %scatter_custom_fusion = f32[32,1920]{0,1:T(8,128)} fusion(s32[5120]{0:T(1024)S(1)} %reshape.805, f32[5120,32]{1,0:T(8,128)} %bitcast.336, f32[]{:T(128)} %constant.12.clone.1), kind=kCustom, calls=%fused_computation.162 | custom fusion | flops 163840 | bytes 246272 | tf_op jit(solution)/shard_map/scatter-add | solution.py:63
  160.7 8.8 collective-permute-start.8
  200.7 90.2 %all-reduce = (f32[8]{0:T(128)S(1)}, f32[8]{0:T(128)S(1)}) all-reduce(f32[8]{0:T(128)S(1)} %get-tuple-element.16, f32[8]{0:T(128)S(1)} %get-tuple-element.15), channel_id=1, replica_groups=mesh['dom'=256] {'dom'}, use_global_device_ids=true, to_apply=%region_8.0 | all-reduce | flops 16 | bytes 128 | tf_op jit(solution)/shard_map/psum | solution.py:116
  309.4 7.8 collective-permute-start.21
  325.6 18.8 %gather_fusion.13 = f32[5120,8]{1,0:T(8,128)} fusion(f32[8,1920]{0,1:T(8,128)} %constant_dynamic-update-slice_fusion.9, s32[5120]{0:T(1024)S(1)} %broadcast_clamp_fusion), kind=kCustom, calls=%fused_computation.13 | custom fusion | bytes 348160 | tf_op jit(solution)/shard_map/gather | solution.py:123
  348.2 7.2 convolution_bitcast_fusion.5
  360.9 29.0 %scatter_custom_fusion.14 = f32[8,1920]{0,1:T(8,128)} fusion(s32[5120]{0:T(1024)S(1)} %reshape.805, f32[5120,8]{1,0:T(8,128)} %copy.192, f32[]{:T(128)} %constant.12.clone.1), kind=kCustom, calls=%fused_computation.159 | custom fusion | flops 40960 | bytes 61952 | tf_op jit(solution)/shard_map/scatter-add | solution.py:63
  391.4 8.7 collective-permute-start.24
  407.1 18.2 %scatter_custom_fusion.43 = f32[576]{0:T(1024)S(1)} fusion(s32[2560]{0:T(1024)S(1)} %reshape.1165, f32[2560]{0:T(1024)S(1)} %reshape.1167, f32[]{:T(128)} %constant.12.clone.1), kind=kCustom, calls=%fused_computation.370 | custom fusion | flops 2560 | bytes 2308 | tf_op jit(solution)/shard_map/scatter-add | solution.py:63
  462.2 8.8 collective-permute-start.33
  479.6 18.8 %gather_fusion.20 = f32[5120,8]{1,0:T(8,128)} fusion(f32[8,1920]{0,1:T(8,128)} %constant_dynamic-update-slice_fusion.16, s32[5120]{0:T(1024)S(1)} %broadcast_clamp_fusion), kind=kCustom, calls=%fused_computation.20 | custom fusion | bytes 348160 | tf_op jit(solution)/shard_map/gather | solution.py:123
  502.2 7.2 convolution_bitcast_fusion.4
  513.2 29.0 %scatter_custom_fusion.21 = f32[8,1920]{0,1:T(8,128)} fusion(s32[5120]{0:T(1024)S(1)} %reshape.805, f32[5120,8]{1,0:T(8,128)} %copy.196, f32[]{:T(128)} %constant.12.clone.1), kind=kCustom, calls=%fused_computation.157 | custom fusion | flops 40960 | bytes 61952 | tf_op jit(solution)/shard_map/scatter-add | solution.py:63
  543.1 11.8 %collective-permute-start.36 = (f32[8,64]{0,1:T(8,128)S(1)}, f32[8,64]{0,1:T(8,128)S(1)}, u32[]{:S(2)}, u32[]{:S(2)}) collective-permute-start(f32[8,64]{0,1:T(8,128)S(1)} %get-tuple-element.48), channel_id=1, source_target_pairs={{0,255},{1,0},{2,1},{3,2},{4,3},{5,4},{6,5},{7,6},{8,7},{9,8},{10,... | collective-permute-start | bytes 6152 | tf_op jit(solution)/shard_map/ppermute | solution.py:17
  599.7 9.2 collective-permute-start.45
  609.0 5.2 collective-permute-start.47
  617.8 18.8 %gather_fusion.27 = f32[5120,8]{1,0:T(8,128)} fusion(f32[8,1920]{0,1:T(8,128)} %constant_dynamic-update-slice_fusion.23, s32[5120]{0:T(1024)S(1)} %broadcast_clamp_fusion), kind=kCustom, calls=%fused_computation.27 | custom fusion | bytes 348160 | tf_op jit(solution)/shard_map/gather | solution.py:123
  640.4 7.2 convolution_bitcast_fusion.3
  651.4 29.0 %scatter_custom_fusion.28 = f32[8,1920]{0,1:T(8,128)} fusion(s32[5120]{0:T(1024)S(1)} %reshape.805, f32[5120,8]{1,0:T(8,128)} %copy.200, f32[]{:T(128)} %constant.12.clone.1), kind=kCustom, calls=%fused_computation.155 | custom fusion | flops 40960 | bytes 61952 | tf_op jit(solution)/shard_map/scatter-add | solution.py:63
  681.3 11.9 %collective-permute-start.48 = (f32[8,64]{0,1:T(8,128)S(1)}, f32[8,64]{0,1:T(8,128)S(1)}, u32[]{:S(2)}, u32[]{:S(2)}) collective-permute-start(f32[8,64]{0,1:T(8,128)S(1)} %get-tuple-element.42), channel_id=1, source_target_pairs={{0,255},{1,0},{2,1},{3,2},{4,3},{5,4},{6,5},{7,6},{8,7},{9,8},{10,... | collective-permute-start | bytes 6152 | tf_op jit(solution)/shard_map/ppermute | solution.py:17
  713.3 8.7 collective-permute-start.62
  731.1 9.4 scatter_custom_fusion.35
  740.5 9.4 scatter_custom_fusion.36
  750.5 6.0 collective-permute-start.54
  760.0 10.8 collective-permute-start.56
  795.6 6.9 collective-permute-start.66
  813.0 11.3 collective-permute-start.69
  828.5 5.2 collective-permute-start.71
  834.8 5.6 gather_fusion.34
  844.2 6.3 convolution_bitcast_fusion.2
  853.6 14.6 %scatter_custom_fusion.50 = f32[8,576]{0,1:T(8,128)S(1)} fusion(s32[2560]{0:T(1024)S(1)} %reshape.1165, f32[2560,8]{1,0:T(8,128)} %copy.204, f32[]{:T(128)} %constant.12.clone.1), kind=kCustom, calls=%fused_computation.172 | custom fusion | flops 20480 | bytes 18944 | tf_op jit(solution)/shard_map/scatter-add | solution.py:63
  868.2 11.6 collective-permute-start.72
  882.2 5.3 collective-permute-start.76
  920.8 7.8 collective-permute-start.81
  947.2 5.7 collective-permute-start.84
  966.3 7.0 collective-permute-start.85
  973.3 7.8 collective-permute-start.87
  989.7 18.8 %gather_fusion.49 = f32[5120,8]{1,0:T(8,128)} fusion(f32[8,1920]{0,1:T(8,128)} %constant_dynamic-update-slice_fusion.44, s32[5120]{0:T(1024)S(1)} %copy-done.10), kind=kCustom, calls=%fused_computation.49 | custom fusion | bytes 348160 | tf_op jit(solution)/shard_map/gather | solution.py:160
  1012.3 7.3 convolution_bitcast_fusion.1
  1027.7 28.6 %scatter_custom_fusion.57 = f32[16,1920]{0,1:T(8,128)S(1)} fusion(s32[5120]{0:T(1024)} %copy-done.16, f32[5120,16]{1,0:T(8,128)} %bitcast.335, f32[]{:T(128)} %constant.12.clone.1), kind=kCustom, calls=%fused_computation.153 | custom fusion | flops 81920 | bytes 123392 | tf_op jit(solution)/shard_map/scatter-add | solution.py:63
  1056.3 8.3 collective-permute-start.90
  1084.6 82.3 %psum.23 = f32[2,24,24]{2,1,0:T(8,128)S(1)} all-reduce(f32[2,24,24]{2,1,0:T(8,128)S(1)} %fusion.101), channel_id=1, replica_groups=mesh['dom'=256] {'dom'}, use_global_device_ids=true, to_apply=%region_70.0 | all-reduce | flops 1152 | bytes 9216 | tf_op jit(solution)/shard_map/psum | solution.py:170
  (516 shorter events, 429.5 us)
Async XLA Ops:
  4.7 52.9 %collective-permute-start = (f32[16,64]{0,1:T(8,128)}, f32[16,64]{0,1:T(8,128)S(1)}, u32[]{:S(2)}, u32[]{:S(2)}) collective-permute-start(f32[16,64]{0,1:T(8,128)} %bitcast.2), channel_id=1, source_target_pairs={{0,1},{1,2},{2,3},{3,4},{4,5},{5,6},{6,7},{7,8},{8,9},{9,10},{10,1... | collective-permute-start | bytes 12296 | tf_op jit(solution)/shard_map/ppermute | solution.py:17
  9.0 54.1 %collective-permute-start.1 = (f32[16,64]{0,1:T(8,128)}, f32[16,64]{0,1:T(8,128)S(1)}, u32[]{:S(2)}, u32[]{:S(2)}) collective-permute-start(f32[16,64]{0,1:T(8,128)} %bitcast.5), channel_id=1, source_target_pairs={{0,255},{1,0},{2,1},{3,2},{4,3},{5,4},{6,5},{7,6},{8,7},{9,8},{10,... | collective-permute-start | bytes 12296 | tf_op jit(solution)/shard_map/ppermute | solution.py:17
  9.8 61.4 %collective-permute-start.2 = (f32[16,64]{0,1:T(8,128)S(1)}, f32[16,64]{0,1:T(8,128)S(1)}, u32[]{:S(2)}, u32[]{:S(2)}) collective-permute-start(f32[16,64]{0,1:T(8,128)S(1)} %bitcast.344), channel_id=1, source_target_pairs={{0,4},{1,5},{2,6},{3,7},{4,8},{5,9},{6,10},{7,11},{8,12},{9,13},{1... | collective-permute-start | bytes 12296 | tf_op jit(solution)/shard_map/ppermute | solution.py:17
  13.2 58.5 %collective-permute-start.3 = (f32[16,64]{0,1:T(8,128)S(1)}, f32[16,64]{0,1:T(8,128)S(1)}, u32[]{:S(2)}, u32[]{:S(2)}) collective-permute-start(f32[16,64]{0,1:T(8,128)S(1)} %bitcast.343), channel_id=1, source_target_pairs={{0,252},{1,253},{2,254},{3,255},{4,0},{5,1},{6,2},{7,3},{8,4},{9,5... | collective-permute-start | bytes 12296 | tf_op jit(solution)/shard_map/ppermute | solution.py:17
  20.7 51.6 %collective-permute-start.4 = (f32[16,64]{0,1:T(8,128)S(1)}, f32[16,64]{0,1:T(8,128)S(1)}, u32[]{:S(2)}, u32[]{:S(2)}) collective-permute-start(f32[16,64]{0,1:T(8,128)S(1)} %bitcast.342), channel_id=1, source_target_pairs={{0,16},{1,17},{2,18},{3,19},{4,20},{5,21},{6,22},{7,23},{8,24},{9,... | collective-permute-start | bytes 12296 | tf_op jit(solution)/shard_map/ppermute | solution.py:17
  57.7 17.9 %collective-permute-start.5 = (f32[16,64]{0,1:T(8,128)}, f32[16,64]{0,1:T(8,128)S(1)}, u32[]{:S(2)}, u32[]{:S(2)}) collective-permute-start(f32[16,64]{0,1:T(8,128)} %bitcast.345), channel_id=1, source_target_pairs={{0,240},{1,241},{2,242},{3,243},{4,244},{5,245},{6,246},{7,247},{8... | collective-permute-start | bytes 12296 | tf_op jit(solution)/shard_map/ppermute | solution.py:17
  63.1 94.9 %collective-permute-start.12 = (f32[1,64]{1,0:T(1,128)}, f32[1,64]{1,0:T(1,128)}, u32[]{:S(2)}, u32[]{:S(2)}) collective-permute-start(f32[1,64]{1,0:T(1,128)} %get-tuple-element.87), channel_id=1, source_target_pairs={{0,255},{1,0},{2,1},{3,2},{4,3},{5,4},{6,5},{7,6},{8,7},{9,8},{10,... | collective-permute-start | bytes 776 | tf_op jit(solution)/shard_map/ppermute | solution.py:17
  71.2 87.3 %collective-permute-start.13 = (f32[1,64]{1,0:T(1,128)}, f32[1,64]{1,0:T(1,128)}, u32[]{:S(2)}, u32[]{:S(2)}) collective-permute-start(f32[1,64]{1,0:T(1,128)} %get-tuple-element.86), channel_id=1, source_target_pairs={{0,1},{1,2},{2,3},{3,4},{4,5},{5,6},{6,7},{7,8},{8,9},{9,10},{10,1... | collective-permute-start | bytes 776 | tf_op jit(solution)/shard_map/ppermute | solution.py:17
  71.8 87.7 %collective-permute-start.14 = (f32[1,64]{1,0:T(1,128)}, f32[1,64]{1,0:T(1,128)}, u32[]{:S(2)}, u32[]{:S(2)}) collective-permute-start(f32[1,64]{1,0:T(1,128)} %get-tuple-element.85), channel_id=1, source_target_pairs={{0,252},{1,253},{2,254},{3,255},{4,0},{5,1},{6,2},{7,3},{8,4},{9,5... | collective-permute-start | bytes 776 | tf_op jit(solution)/shard_map/ppermute | solution.py:17
  72.4 88.3 %collective-permute-start.15 = (f32[1,64]{1,0:T(1,128)}, f32[1,64]{1,0:T(1,128)}, u32[]{:S(2)}, u32[]{:S(2)}) collective-permute-start(f32[1,64]{1,0:T(1,128)} %get-tuple-element.84), channel_id=1, source_target_pairs={{0,4},{1,5},{2,6},{3,7},{4,8},{5,9},{6,10},{7,11},{8,12},{9,13},{1... | collective-permute-start | bytes 776 | tf_op jit(solution)/shard_map/ppermute | solution.py:17
  159.5 24.2 %collective-permute-start.7 = (f32[32,64]{0,1:T(8,128)S(1)}, f32[32,64]{0,1:T(8,128)S(1)}, u32[]{:S(2)}, u32[]{:S(2)}) collective-permute-start(f32[32,64]{0,1:T(8,128)S(1)} %get-tuple-element.59), channel_id=1, source_target_pairs={{0,1},{1,2},{2,3},{3,4},{4,5},{5,6},{6,7},{7,8},{8,9},{9,10},{10,1... | collective-permute-start | bytes 24584 | tf_op jit(solution)/shard_map/ppermute | solution.py:17
  160.7 25.9 %collective-permute-start.8 = (f32[32,64]{0,1:T(8,128)S(1)}, f32[32,64]{0,1:T(8,128)}, u32[]{:S(2)}, u32[]{:S(2)}) collective-permute-start(f32[32,64]{0,1:T(8,128)S(1)} %get-tuple-element.58), channel_id=1, source_target_pairs={{0,252},{1,253},{2,254},{3,255},{4,0},{5,1},{6,2},{7,3},{8,4},{9,5... | collective-permute-start | bytes 24584 | tf_op jit(solution)/shard_map/ppermute | solution.py:17
  169.5 20.2 %collective-permute-start.9 = (f32[32,64]{0,1:T(8,128)S(1)}, f32[32,64]{0,1:T(8,128)}, u32[]{:S(2)}, u32[]{:S(2)}) collective-permute-start(f32[32,64]{0,1:T(8,128)S(1)} %get-tuple-element.57), channel_id=1, source_target_pairs={{0,4},{1,5},{2,6},{3,7},{4,8},{5,9},{6,10},{7,11},{8,12},{9,13},{1... | collective-permute-start | bytes 24584 | tf_op jit(solution)/shard_map/ppermute | solution.py:17
  169.5 23.3 %collective-permute-start.10 = (f32[32,64]{0,1:T(8,128)S(1)}, f32[32,64]{0,1:T(8,128)}, u32[]{:S(2)}, u32[]{:S(2)}) collective-permute-start(f32[32,64]{0,1:T(8,128)S(1)} %get-tuple-element.56), channel_id=1, source_target_pairs={{0,240},{1,241},{2,242},{3,243},{4,244},{5,245},{6,246},{7,247},{8... | collective-permute-start | bytes 24584 | tf_op jit(solution)/shard_map/ppermute | solution.py:17
  170.0 25.9 %collective-permute-start.11 = (f32[32,64]{0,1:T(8,128)S(1)}, f32[32,64]{0,1:T(8,128)S(1)}, u32[]{:S(2)}, u32[]{:S(2)}) collective-permute-start(f32[32,64]{0,1:T(8,128)S(1)} %get-tuple-element.55), channel_id=1, source_target_pairs={{0,16},{1,17},{2,18},{3,19},{4,20},{5,21},{6,22},{7,23},{8,24},{9,... | collective-permute-start | bytes 24584 | tf_op jit(solution)/shard_map/ppermute | solution.py:17
  295.7 21.5 %collective-permute-start.18 = (f32[8,64]{0,1:T(8,128)S(1)}, f32[8,64]{0,1:T(8,128)S(1)}, u32[]{:S(2)}, u32[]{:S(2)}) collective-permute-start(f32[8,64]{0,1:T(8,128)S(1)} %bitcast.370), channel_id=1, source_target_pairs={{0,1},{1,2},{2,3},{3,4},{4,5},{5,6},{6,7},{7,8},{8,9},{9,10},{10,1... | collective-permute-start | bytes 6152 | tf_op jit(solution)/shard_map/ppermute | solution.py:17
  400.0 30.5 %collective-permute-start.25 = (f32[8,64]{0,1:T(8,128)}, f32[8,64]{0,1:T(8,128)}, u32[]{:S(2)}, u32[]{:S(2)}) collective-permute-start(f32[8,64]{0,1:T(8,128)} %get-tuple-element.53), channel_id=1, source_target_pairs={{0,1},{1,2},{2,3},{3,4},{4,5},{5,6},{6,7},{7,8},{8,9},{9,10},{10,1... | collective-permute-start | bytes 6152 | tf_op jit(solution)/shard_map/ppermute | solution.py:17
  400.0 33.6 %collective-permute-start.26 = (f32[8,64]{0,1:T(8,128)}, f32[8,64]{0,1:T(8,128)}, u32[]{:S(2)}, u32[]{:S(2)}) collective-permute-start(f32[8,64]{0,1:T(8,128)} %get-tuple-element.52), channel_id=1, source_target_pairs={{0,252},{1,253},{2,254},{3,255},{4,0},{5,1},{6,2},{7,3},{8,4},{9,5... | collective-permute-start | bytes 6152 | tf_op jit(solution)/shard_map/ppermute | solution.py:17
  403.0 33.7 %collective-permute-start.27 = (f32[8,64]{0,1:T(8,128)S(1)}, f32[8,64]{0,1:T(8,128)}, u32[]{:S(2)}, u32[]{:S(2)}) collective-permute-start(f32[8,64]{0,1:T(8,128)S(1)} %get-tuple-element.51), channel_id=1, source_target_pairs={{0,4},{1,5},{2,6},{3,7},{4,8},{5,9},{6,10},{7,11},{8,12},{9,13},{1... | collective-permute-start | bytes 6152 | tf_op jit(solution)/shard_map/ppermute | solution.py:17
  403.0 36.8 %collective-permute-start.28 = (f32[8,64]{0,1:T(8,128)S(1)}, f32[8,64]{0,1:T(8,128)}, u32[]{:S(2)}, u32[]{:S(2)}) collective-permute-start(f32[8,64]{0,1:T(8,128)S(1)} %get-tuple-element.50), channel_id=1, source_target_pairs={{0,240},{1,241},{2,242},{3,243},{4,244},{5,245},{6,246},{7,247},{8... | collective-permute-start | bytes 6152 | tf_op jit(solution)/shard_map/ppermute | solution.py:17
  406.4 36.5 %collective-permute-start.29 = (f32[8,64]{0,1:T(8,128)S(1)}, f32[8,64]{0,1:T(8,128)}, u32[]{:S(2)}, u32[]{:S(2)}) collective-permute-start(f32[8,64]{0,1:T(8,128)S(1)} %get-tuple-element.49), channel_id=1, source_target_pairs={{0,16},{1,17},{2,18},{3,19},{4,20},{5,21},{6,22},{7,23},{8,24},{9,... | collective-permute-start | bytes 6152 | tf_op jit(solution)/shard_map/ppermute | solution.py:17
  450.5 20.4 %collective-permute-start.30 = (f32[8,64]{0,1:T(8,128)S(1)}, f32[8,64]{0,1:T(8,128)S(1)}, u32[]{:S(2)}, u32[]{:S(2)}) collective-permute-start(f32[8,64]{0,1:T(8,128)S(1)} %bitcast.367), channel_id=1, source_target_pairs={{0,1},{1,2},{2,3},{3,4},{4,5},{5,6},{6,7},{7,8},{8,9},{9,10},{10,1... | collective-permute-start | bytes 6152 | tf_op jit(solution)/shard_map/ppermute | solution.py:17
  543.1 18.7 %collective-permute-start.36 = (f32[8,64]{0,1:T(8,128)S(1)}, f32[8,64]{0,1:T(8,128)S(1)}, u32[]{:S(2)}, u32[]{:S(2)}) collective-permute-start(f32[8,64]{0,1:T(8,128)S(1)} %get-tuple-element.48), channel_id=1, source_target_pairs={{0,255},{1,0},{2,1},{3,2},{4,3},{5,4},{6,5},{7,6},{8,7},{9,8},{10,... | collective-permute-start | bytes 6152 | tf_op jit(solution)/shard_map/ppermute | solution.py:17
  558.2 18.5 %collective-permute-start.40 = (f32[8,64]{0,1:T(8,128)S(1)}, f32[8,64]{0,1:T(8,128)S(1)}, u32[]{:S(2)}, u32[]{:S(2)}) collective-permute-start(f32[8,64]{0,1:T(8,128)S(1)} %get-tuple-element.44), channel_id=1, source_target_pairs={{0,240},{1,241},{2,242},{3,243},{4,244},{5,245},{6,246},{7,247},{8... | collective-permute-start | bytes 6152 | tf_op jit(solution)/shard_map/ppermute | solution.py:17
  562.4 17.2 %collective-permute-start.41 = (f32[8,64]{0,1:T(8,128)S(1)}, f32[8,64]{0,1:T(8,128)S(1)}, u32[]{:S(2)}, u32[]{:S(2)}) collective-permute-start(f32[8,64]{0,1:T(8,128)S(1)} %get-tuple-element.43), channel_id=1, source_target_pairs={{0,16},{1,17},{2,18},{3,19},{4,20},{5,21},{6,22},{7,23},{8,24},{9,... | collective-permute-start | bytes 6152 | tf_op jit(solution)/shard_map/ppermute | solution.py:17
  588.4 20.5 %collective-permute-start.42 = (f32[8,64]{0,1:T(8,128)}, f32[8,64]{0,1:T(8,128)S(1)}, u32[]{:S(2)}, u32[]{:S(2)}) collective-permute-start(f32[8,64]{0,1:T(8,128)} %bitcast.69), channel_id=1, source_target_pairs={{0,1},{1,2},{2,3},{3,4},{4,5},{5,6},{6,7},{7,8},{8,9},{9,10},{10,1... | collective-permute-start | bytes 6152 | tf_op jit(solution)/shard_map/ppermute | solution.py:17
  681.3 18.8 %collective-permute-start.48 = (f32[8,64]{0,1:T(8,128)S(1)}, f32[8,64]{0,1:T(8,128)S(1)}, u32[]{:S(2)}, u32[]{:S(2)}) collective-permute-start(f32[8,64]{0,1:T(8,128)S(1)} %get-tuple-element.42), channel_id=1, source_target_pairs={{0,255},{1,0},{2,1},{3,2},{4,3},{5,4},{6,5},{7,6},{8,7},{9,8},{10,... | collective-permute-start | bytes 6152 | tf_op jit(solution)/shard_map/ppermute | solution.py:17
  696.2 17.1 %collective-permute-start.51 = (f32[8,64]{0,1:T(8,128)S(1)}, f32[8,64]{0,1:T(8,128)S(1)}, u32[]{:S(2)}, u32[]{:S(2)}) collective-permute-start(f32[8,64]{0,1:T(8,128)S(1)} %get-tuple-element.39), channel_id=1, source_target_pairs={{0,4},{1,5},{2,6},{3,7},{4,8},{5,9},{6,10},{7,11},{8,12},{9,13},{1... | collective-permute-start | bytes 6152 | tf_op jit(solution)/shard_map/ppermute | solution.py:17
  696.2 28.8 %collective-permute-start.52 = (f32[8,64]{0,1:T(8,128)S(1)}, f32[8,64]{0,1:T(8,128)S(1)}, u32[]{:S(2)}, u32[]{:S(2)}) collective-permute-start(f32[8,64]{0,1:T(8,128)S(1)} %get-tuple-element.38), channel_id=1, source_target_pairs={{0,240},{1,241},{2,242},{3,243},{4,244},{5,245},{6,246},{7,247},{8... | collective-permute-start | bytes 6152 | tf_op jit(solution)/shard_map/ppermute | solution.py:17
  700.1 27.9 %collective-permute-start.53 = (f32[8,64]{0,1:T(8,128)S(1)}, f32[8,64]{0,1:T(8,128)S(1)}, u32[]{:S(2)}, u32[]{:S(2)}) collective-permute-start(f32[8,64]{0,1:T(8,128)S(1)} %get-tuple-element.37), channel_id=1, source_target_pairs={{0,16},{1,17},{2,18},{3,19},{4,20},{5,21},{6,22},{7,23},{8,24},{9,... | collective-permute-start | bytes 6152 | tf_op jit(solution)/shard_map/ppermute | solution.py:17
  705.5 51.0 %collective-permute-start.60 = (f32[1,32]{1,0:T(1,128)}, f32[1,32]{1,0:T(1,128)}, u32[]{:S(2)}, u32[]{:S(2)}) collective-permute-start(f32[1,32]{1,0:T(1,128)} %get-tuple-element.105), channel_id=1, source_target_pairs={{0,255},{1,0},{2,1},{3,2},{4,3},{5,4},{6,5},{7,6},{8,7},{9,8},{10,... | collective-permute-start | bytes 392 | tf_op jit(solution)/shard_map/ppermute | solution.py:17
  709.9 47.6 %collective-permute-start.61 = (f32[1,32]{1,0:T(1,128)}, f32[1,32]{1,0:T(1,128)}, u32[]{:S(2)}, u32[]{:S(2)}) collective-permute-start(f32[1,32]{1,0:T(1,128)} %get-tuple-element.104), channel_id=1, source_target_pairs={{0,1},{1,2},{2,3},{3,4},{4,5},{5,6},{6,7},{7,8},{8,9},{9,10},{10,1... | collective-permute-start | bytes 392 | tf_op jit(solution)/shard_map/ppermute | solution.py:17
  713.3 46.6 %collective-permute-start.62 = (f32[1,32]{1,0:T(1,128)}, f32[1,32]{1,0:T(1,128)}, u32[]{:S(2)}, u32[]{:S(2)}) collective-permute-start(f32[1,32]{1,0:T(1,128)} %get-tuple-element.103), channel_id=1, source_target_pairs={{0,252},{1,253},{2,254},{3,255},{4,0},{5,1},{6,2},{7,3},{8,4},{9,5... | collective-permute-start | bytes 392 | tf_op jit(solution)/shard_map/ppermute | solution.py:17
  725.0 34.9 %collective-permute-start.63 = (f32[1,32]{1,0:T(1,128)}, f32[1,32]{1,0:T(1,128)}, u32[]{:S(2)}, u32[]{:S(2)}) collective-permute-start(f32[1,32]{1,0:T(1,128)} %get-tuple-element.102), channel_id=1, source_target_pairs={{0,4},{1,5},{2,6},{3,7},{4,8},{5,9},{6,10},{7,11},{8,12},{9,13},{1... | collective-permute-start | bytes 392 | tf_op jit(solution)/shard_map/ppermute | solution.py:17
  750.5 20.3 %collective-permute-start.54 = (f32[8,32]{0,1:T(8,128)}, f32[8,32]{0,1:T(8,128)}, u32[]{:S(2)}, u32[]{:S(2)}) collective-permute-start(f32[8,32]{0,1:T(8,128)} %get-tuple-element.72), channel_id=1, source_target_pairs={{0,255},{1,0},{2,1},{3,2},{4,3},{5,4},{6,5},{7,6},{8,7},{9,8},{10,... | collective-permute-start | bytes 3080 | tf_op jit(solution)/shard_map/ppermute | solution.py:17
  759.9 19.3 %collective-permute-start.55 = (f32[8,32]{0,1:T(8,128)}, f32[8,32]{0,1:T(8,128)}, u32[]{:S(2)}, u32[]{:S(2)}) collective-permute-start(f32[8,32]{0,1:T(8,128)} %get-tuple-element.71), channel_id=1, source_target_pairs={{0,1},{1,2},{2,3},{3,4},{4,5},{5,6},{6,7},{7,8},{8,9},{9,10},{10,1... | collective-permute-start | bytes 3080 | tf_op jit(solution)/shard_map/ppermute | solution.py:17
  760.0 21.7 %collective-permute-start.56 = (f32[8,32]{0,1:T(8,128)S(1)}, f32[8,32]{0,1:T(8,128)}, u32[]{:S(2)}, u32[]{:S(2)}) collective-permute-start(f32[8,32]{0,1:T(8,128)S(1)} %get-tuple-element.70), channel_id=1, source_target_pairs={{0,252},{1,253},{2,254},{3,255},{4,0},{5,1},{6,2},{7,3},{8,4},{9,5... | collective-permute-start | bytes 3080 | tf_op jit(solution)/shard_map/ppermute | solution.py:17
  770.9 18.2 %collective-permute-start.59 = (f32[8,32]{0,1:T(8,128)S(1)}, f32[8,32]{0,1:T(8,128)}, u32[]{:S(2)}, u32[]{:S(2)}) collective-permute-start(f32[8,32]{0,1:T(8,128)S(1)} %get-tuple-element.67), channel_id=1, source_target_pairs={{0,16},{1,17},{2,18},{3,19},{4,20},{5,21},{6,22},{7,23},{8,24},{9,... | collective-permute-start | bytes 3080 | tf_op jit(solution)/shard_map/ppermute | solution.py:17
  795.6 32.9 %collective-permute-start.66 = (f32[8,32]{0,1:T(8,128)}, f32[8,32]{0,1:T(8,128)S(1)}, u32[]{:S(2)}, u32[]{:S(2)}) collective-permute-start(f32[8,32]{0,1:T(8,128)} %bitcast.112), channel_id=1, source_target_pairs={{0,1},{1,2},{2,3},{3,4},{4,5},{5,6},{6,7},{7,8},{8,9},{9,10},{10,1... | collective-permute-start | bytes 3080 | tf_op jit(solution)/shard_map/ppermute | solution.py:17
  808.6 25.1 %collective-permute-start.67 = (f32[8,32]{0,1:T(8,128)}, f32[8,32]{0,1:T(8,128)}, u32[]{:S(2)}, u32[]{:S(2)}) collective-permute-start(f32[8,32]{0,1:T(8,128)} %bitcast.113), channel_id=1, source_target_pairs={{0,255},{1,0},{2,1},{3,2},{4,3},{5,4},{6,5},{7,6},{8,7},{9,8},{10,... | collective-permute-start | bytes 3080 | tf_op jit(solution)/shard_map/ppermute | solution.py:17
  810.8 23.6 %collective-permute-start.68 = (f32[8,32]{0,1:T(8,128)}, f32[8,32]{0,1:T(8,128)S(1)}, u32[]{:S(2)}, u32[]{:S(2)}) collective-permute-start(f32[8,32]{0,1:T(8,128)} %bitcast.114), channel_id=1, source_target_pairs={{0,4},{1,5},{2,6},{3,7},{4,8},{5,9},{6,10},{7,11},{8,12},{9,13},{1... | collective-permute-start | bytes 3080 | tf_op jit(solution)/shard_map/ppermute | solution.py:17
  813.0 21.4 %collective-permute-start.69 = (f32[8,32]{0,1:T(8,128)}, f32[8,32]{0,1:T(8,128)S(1)}, u32[]{:S(2)}, u32[]{:S(2)}) collective-permute-start(f32[8,32]{0,1:T(8,128)} %bitcast.115), channel_id=1, source_target_pairs={{0,252},{1,253},{2,254},{3,255},{4,0},{5,1},{6,2},{7,3},{8,4},{9,5... | collective-permute-start | bytes 3080 | tf_op jit(solution)/shard_map/ppermute | solution.py:17
  868.2 19.3 %collective-permute-start.72 = (f32[8,32]{0,1:T(8,128)S(1)}, f32[8,32]{0,1:T(8,128)S(1)}, u32[]{:S(2)}, u32[]{:S(2)}) collective-permute-start(f32[8,32]{0,1:T(8,128)S(1)} %get-tuple-element.66), channel_id=1, source_target_pairs={{0,255},{1,0},{2,1},{3,2},{4,3},{5,4},{6,5},{7,6},{8,7},{9,8},{10,... | collective-permute-start | bytes 3080 | tf_op jit(solution)/shard_map/ppermute | solution.py:17
  879.9 16.4 %collective-permute-start.75 = (f32[8,32]{0,1:T(8,128)S(1)}, f32[8,32]{0,1:T(8,128)}, u32[]{:S(2)}, u32[]{:S(2)}) collective-permute-start(f32[8,32]{0,1:T(8,128)S(1)} %get-tuple-element.63), channel_id=1, source_target_pairs={{0,4},{1,5},{2,6},{3,7},{4,8},{5,9},{6,10},{7,11},{8,12},{9,13},{1... | collective-permute-start | bytes 3080 | tf_op jit(solution)/shard_map/ppermute | solution.py:17
  882.2 16.5 %collective-permute-start.76 = (f32[8,32]{0,1:T(8,128)S(1)}, f32[8,32]{0,1:T(8,128)}, u32[]{:S(2)}, u32[]{:S(2)}) collective-permute-start(f32[8,32]{0,1:T(8,128)S(1)} %get-tuple-element.62), channel_id=1, source_target_pairs={{0,240},{1,241},{2,242},{3,243},{4,244},{5,245},{6,246},{7,247},{8... | collective-permute-start | bytes 3080 | tf_op jit(solution)/shard_map/ppermute | solution.py:17
  907.9 20.7 %collective-permute-start.78 = (f32[8,32]{0,1:T(8,128)}, f32[8,32]{0,1:T(8,128)}, u32[]{:S(2)}, u32[]{:S(2)}) collective-permute-start(f32[8,32]{0,1:T(8,128)} %bitcast.128), channel_id=1, source_target_pairs={{0,1},{1,2},{2,3},{3,4},{4,5},{5,6},{6,7},{7,8},{8,9},{9,10},{10,1... | collective-permute-start | bytes 3080 | tf_op jit(solution)/shard_map/ppermute | solution.py:17
  947.2 33.9 %collective-permute-start.84 = (f32[8,64]{0,1:T(8,128)S(1)}, f32[8,64]{0,1:T(8,128)S(1)}, u32[]{:S(2)}, u32[]{:S(2)}) collective-permute-start(f32[8,64]{0,1:T(8,128)S(1)} %bitcast.369), channel_id=1, source_target_pairs={{0,1},{1,2},{2,3},{3,4},{4,5},{5,6},{6,7},{7,8},{8,9},{9,10},{10,1... | collective-permute-start | bytes 6152 | tf_op jit(solution)/shard_map/ppermute | solution.py:17
  966.3 20.4 %collective-permute-start.85 = (f32[8,64]{0,1:T(8,128)}, f32[8,64]{0,1:T(8,128)S(1)}, u32[]{:S(2)}, u32[]{:S(2)}) collective-permute-start(f32[8,64]{0,1:T(8,128)} %bitcast.139), channel_id=1, source_target_pairs={{0,255},{1,0},{2,1},{3,2},{4,3},{5,4},{6,5},{7,6},{8,7},{9,8},{10,... | collective-permute-start | bytes 6152 | tf_op jit(solution)/shard_map/ppermute | solution.py:17
  (105 other events, 5205.4 us)
where the time goes:
time: 1180 us; the launch traced here: 1170 us
  other arithmetic  374 us (32%)
  local copies, waits for them, and re-layouts  290 us (25%)
  starting transfers between devices  266 us (23%)
  blocking collectives  173 us (15%)
  matrix products  61.6 us (5%)
    ppermute x96, starting transfers between devices, from_behind(): lax.ppermute(shard, axis, [(i, (i + by) % length) for i in range(length)])  266 us
    scatter-add x8, other arithmetic, scatter_local(): jnp.zeros((terms.shape[0], length), jnp.float32).at[:, connect].add(terms)  205 us
    psum x1, blocking collectives, shards(): lax.psum((jnp.sum(x_block * stiff_x, axis=1), jnp.sum(x_block * mass_x, a...  90.2 us
    scatter-add x36, other arithmetic, edge_return(): total = total.at[:, send_edge[direction]].add(back)  87 us
    psum x1, blocking collectives, shards(): lax.psum(arrange(jnp.stack([stiff_part, mass_part]), w_rows, modes), 'dom')  82.3 us
    gather x6, local copies, waits for them, and re-layouts, stiff_image(): values = edge_extend(vectors, send_edge)[:, elem_edge]  67.8 us
    dot_general x8, matrix products, element_terms(): return jnp.einsum('jke,cke->cje', matrices, values, precision=highest)  56.3 us
    gather x30, local copies, waits for them, and re-layouts, edge_extend(): outgoing = values[:, send_edge[direction]]  54.6 us
  transfers between devices with their start and end apart: 96, of which 3 were waited for; matrix products, arithmetic and copies ran while one was open for 31% of the time, Pallas kernels for 0%

commit v1 on v0

--- a/solution.py
+++ b/solution.py
@@ -167,7 +167,8 @@
     w_rows = jnp.stack([inner_rows(w_images[:modes], basis), inner_rows(w_images[modes:], basis)])
     stiff_part = inner_rows(pair, jnp.concatenate([stiff_x, stiff_p], axis=0))
     mass_part = inner_rows(pair, jnp.concatenate([mass_x, mass_p], axis=0))
-    full_gram = lax.psum(arrange(jnp.stack([stiff_part, mass_part]), w_rows, modes), "dom")
+    shard_in = arrange(jnp.stack([stiff_part, mass_part]), w_rows, modes)
+    full_gram = jnp.sum(lax.all_gather(shard_in, "dom"), 0)
     total_edges = owned_edges * lax.axis_size("dom")
     return (w_block, full_gram[0] / total_edges, full_gram[1] / total_edges)
 

time: 1180 us -> 1240 us (1.051)
  waiting for transfers between devices: 2.27 us -> 121 us
  blocking collectives: 173 us -> 90.3 us
  between operations: 2.21 us -> 15.6 us
    all_gather x0 -> x1, waiting for transfers between devices: none -> 119 us  [shards(): full_gram = jnp.sum(lax.all_gather(shard_in, 'dom'), 0)]
    psum x1 -> x0, blocking collectives: 82.3 us -> none  [shards(): lax.psum(arrange(jnp.stack([stiff_part, mass_part]), w_rows, modes), 'dom')]
  transfers between devices with their start and end apart: 96 -> 97, of which waited for: 3 -> 4; matrix products, arithmetic and copies ran while one was open for 31% -> 30% of each run, Pallas kernels for 0% -> 0%
where the time goes in v1:
time: 1240 us; the launch traced here: 1220 us
  other arithmetic  378 us (30%)
  local copies, waits for them, and re-layouts  290 us (23%)
  starting transfers between devices  266 us (21%)
  waiting for transfers between devices  121 us (10%)
  blocking collectives  90.3 us (7%)
  matrix products  61.6 us (5%)
  between operations  15.6 us (1%)
    ppermute x96, starting transfers between devices, from_behind(): lax.ppermute(shard, axis, [(i, (i + by) % length) for i in range(length)])  266 us
    scatter-add x8, other arithmetic, scatter_local(): jnp.zeros((terms.shape[0], length), jnp.float32).at[:, connect].add(terms)  205 us
    all_gather x1, waiting for transfers between devices, shards(): full_gram = jnp.sum(lax.all_gather(shard_in, 'dom'), 0)  119 us
    psum x1, blocking collectives, shards(): lax.psum((jnp.sum(x_block * stiff_x, axis=1), jnp.sum(x_block * mass_x, a...  90.3 us
    scatter-add x36, other arithmetic, edge_return(): total = total.at[:, send_edge[direction]].add(back)  87 us
    gather x6, local copies, waits for them, and re-layouts, stiff_image(): values = edge_extend(vectors, send_edge)[:, elem_edge]  67.8 us
    dot_general x8, matrix products, element_terms(): return jnp.einsum('jke,cke->cje', matrices, values, precision=highest)  56.3 us
    gather x30, local copies, waits for them, and re-layouts, edge_extend(): outgoing = values[:, send_edge[direction]]  54.6 us
  transfers between devices with their start and end apart: 97, of which 4 were waited for; matrix products, arithmetic and copies ran while one was open for 30% of the time, Pallas kernels for 0%

profile of v1, /device:TPU:1, one launch (start us, length us, event | category | flops | bytes accessed | tf_op | source)
XLA Modules:
  0.0 1221.8 jit_solution(2092807653618534598)
XLA Ops:
  19.8 6.9 collective-permute-start.3
  28.6 27.5 %scatter_custom_fusion.7 = f32[1920]{0:T(1024)S(1)} fusion(s32[5120]{0:T(1024)S(1)} %reshape.805, f32[5120]{0:T(1024)S(1)} %reshape.865, f32[]{:T(128)} %constant.12.clone.1), kind=kCustom, calls=%fused_computation.356 | custom fusion | flops 5120 | bytes 7684 | tf_op jit(solution)/shard_map/scatter-add | solution.py:63
  69.7 7.5 collective-permute-start.12
  82.7 18.8 %gather_fusion.6 = f32[5120,16]{1,0:T(8,128)} fusion(f32[16,1920]{0,1:T(8,128)} %constant_dynamic-update-slice_fusion.2, s32[5120]{0:T(1024)S(1)} %broadcast_clamp_fusion), kind=kCustom, calls=%fused_computation.6 | custom fusion | bytes 675840 | tf_op jit(solution)/shard_map/gather | solution.py:99
  105.5 7.3 fusion.7
  115.4 8.9 fusion.4
  132.4 29.0 %scatter_custom_fusion = f32[32,1920]{0,1:T(8,128)} fusion(s32[5120]{0:T(1024)S(1)} %reshape.805, f32[5120,32]{1,0:T(8,128)} %bitcast.338, f32[]{:T(128)} %constant.12.clone.1), kind=kCustom, calls=%fused_computation.162 | custom fusion | flops 163840 | bytes 246272 | tf_op jit(solution)/shard_map/scatter-add | solution.py:63
  167.3 8.8 collective-permute-start.8
  207.3 90.3 %all-reduce = (f32[8]{0:T(128)S(1)}, f32[8]{0:T(128)S(1)}) all-reduce(f32[8]{0:T(128)S(1)} %get-tuple-element.16, f32[8]{0:T(128)S(1)} %get-tuple-element.15), channel_id=1, replica_groups=mesh['dom'=256] {'dom'}, use_global_device_ids=true, to_apply=%region_8.0 | all-reduce | flops 16 | bytes 128 | tf_op jit(solution)/shard_map/psum | solution.py:116
  316.0 7.8 collective-permute-start.21
  332.2 18.8 %gather_fusion.13 = f32[5120,8]{1,0:T(8,128)} fusion(f32[8,1920]{0,1:T(8,128)} %constant_dynamic-update-slice_fusion.9, s32[5120]{0:T(1024)S(1)} %broadcast_clamp_fusion), kind=kCustom, calls=%fused_computation.13 | custom fusion | bytes 348160 | tf_op jit(solution)/shard_map/gather | solution.py:123
  354.8 7.2 convolution_bitcast_fusion.5
  367.4 29.0 %scatter_custom_fusion.14 = f32[8,1920]{0,1:T(8,128)} fusion(s32[5120]{0:T(1024)S(1)} %reshape.805, f32[5120,8]{1,0:T(8,128)} %copy.192, f32[]{:T(128)} %constant.12.clone.1), kind=kCustom, calls=%fused_computation.159 | custom fusion | flops 40960 | bytes 61952 | tf_op jit(solution)/shard_map/scatter-add | solution.py:63
  397.9 8.7 collective-permute-start.24
  413.7 18.2 %scatter_custom_fusion.43 = f32[576]{0:T(1024)S(1)} fusion(s32[2560]{0:T(1024)S(1)} %reshape.1165, f32[2560]{0:T(1024)S(1)} %reshape.1167, f32[]{:T(128)} %constant.12.clone.1), kind=kCustom, calls=%fused_computation.370 | custom fusion | flops 2560 | bytes 2308 | tf_op jit(solution)/shard_map/scatter-add | solution.py:63
  468.7 8.8 collective-permute-start.33
  486.2 18.8 %gather_fusion.20 = f32[5120,8]{1,0:T(8,128)} fusion(f32[8,1920]{0,1:T(8,128)} %constant_dynamic-update-slice_fusion.16, s32[5120]{0:T(1024)S(1)} %broadcast_clamp_fusion), kind=kCustom, calls=%fused_computation.20 | custom fusion | bytes 348160 | tf_op jit(solution)/shard_map/gather | solution.py:123
  508.8 7.2 convolution_bitcast_fusion.4
  519.8 29.0 %scatter_custom_fusion.21 = f32[8,1920]{0,1:T(8,128)} fusion(s32[5120]{0:T(1024)S(1)} %reshape.805, f32[5120,8]{1,0:T(8,128)} %copy.196, f32[]{:T(128)} %constant.12.clone.1), kind=kCustom, calls=%fused_computation.157 | custom fusion | flops 40960 | bytes 61952 | tf_op jit(solution)/shard_map/scatter-add | solution.py:63
  549.7 11.8 collective-permute-start.36
  606.3 9.2 collective-permute-start.45
  615.5 5.2 collective-permute-start.47
  624.4 18.8 %gather_fusion.27 = f32[5120,8]{1,0:T(8,128)} fusion(f32[8,1920]{0,1:T(8,128)} %constant_dynamic-update-slice_fusion.23, s32[5120]{0:T(1024)S(1)} %broadcast_clamp_fusion), kind=kCustom, calls=%fused_computation.27 | custom fusion | bytes 348160 | tf_op jit(solution)/shard_map/gather | solution.py:123
  646.9 7.2 convolution_bitcast_fusion.3
  658.0 29.0 %scatter_custom_fusion.28 = f32[8,1920]{0,1:T(8,128)} fusion(s32[5120]{0:T(1024)S(1)} %reshape.805, f32[5120,8]{1,0:T(8,128)} %copy.200, f32[]{:T(128)} %constant.12.clone.1), kind=kCustom, calls=%fused_computation.155 | custom fusion | flops 40960 | bytes 61952 | tf_op jit(solution)/shard_map/scatter-add | solution.py:63
  687.9 11.9 collective-permute-start.48
  719.9 8.7 collective-permute-start.62
  737.7 9.4 scatter_custom_fusion.35
  747.1 9.4 scatter_custom_fusion.36
  757.1 6.0 collective-permute-start.54
  766.6 10.8 collective-permute-start.56
  802.1 6.9 collective-permute-start.66
  819.6 11.3 collective-permute-start.69
  835.1 5.2 collective-permute-start.71
  841.3 5.6 gather_fusion.34
  850.8 6.3 convolution_bitcast_fusion.2
  860.2 14.6 %scatter_custom_fusion.50 = f32[8,576]{0,1:T(8,128)S(1)} fusion(s32[2560]{0:T(1024)S(1)} %reshape.1165, f32[2560,8]{1,0:T(8,128)} %copy.204, f32[]{:T(128)} %constant.12.clone.1), kind=kCustom, calls=%fused_computation.172 | custom fusion | flops 20480 | bytes 18944 | tf_op jit(solution)/shard_map/scatter-add | solution.py:63
  874.8 11.6 collective-permute-start.72
  888.8 5.3 collective-permute-start.76
  927.4 7.8 collective-permute-start.81
  953.8 5.7 collective-permute-start.84
  972.9 7.0 collective-permute-start.85
  979.9 7.8 collective-permute-start.87
  996.3 18.8 %gather_fusion.49 = f32[5120,8]{1,0:T(8,128)} fusion(f32[8,1920]{0,1:T(8,128)} %constant_dynamic-update-slice_fusion.44, s32[5120]{0:T(1024)S(1)} %copy-done.10), kind=kCustom, calls=%fused_computation.49 | custom fusion | bytes 348160 | tf_op jit(solution)/shard_map/gather | solution.py:160
  1018.9 7.3 convolution_bitcast_fusion.1
  1034.3 28.6 %scatter_custom_fusion.57 = f32[16,1920]{0,1:T(8,128)S(1)} fusion(s32[5120]{0:T(1024)} %copy-done.16, f32[5120,16]{1,0:T(8,128)} %bitcast.337, f32[]{:T(128)} %constant.12.clone.1), kind=kCustom, calls=%fused_computation.153 | custom fusion | flops 81920 | bytes 123392 | tf_op jit(solution)/shard_map/scatter-add | solution.py:63
  1062.9 8.3 collective-permute-start.90
  1091.8 118.8 %all-gather.3.cloned.1.call-done = f32[512,24,24]{2,1,0:T(8,128)} async-done(((f32[2,24,24]{2,1,0:T(8,128)}), f32[512,24,24]{2,1,0:T(8,128)}) %all-gather.3.cloned.1.call-update) | async-done | bytes 1179664 | tf_op jit(solution)/shard_map/all_gather | solution.py:171
  (519 shorter events, 433.5 us)
Async XLA Ops:
  7.2 1203.4 %all-gather.3.cloned.1.call-start = ((), (), s32[]{:S(2)}) async-start(), calls=%async_computation | async-start | bytes 6316032 | tf_op jit(solution)/shard_map/all_gather | solution.py:171
  11.3 52.9 %collective-permute-start = (f32[16,64]{0,1:T(8,128)}, f32[16,64]{0,1:T(8,128)S(1)}, u32[]{:S(2)}, u32[]{:S(2)}) collective-permute-start(f32[16,64]{0,1:T(8,128)} %bitcast.2), channel_id=1, source_target_pairs={{0,1},{1,2},{2,3},{3,4},{4,5},{5,6},{6,7},{7,8},{8,9},{9,10},{10,1... | collective-permute-start | bytes 12296 | tf_op jit(solution)/shard_map/ppermute | solution.py:17
  15.5 54.1 %collective-permute-start.1 = (f32[16,64]{0,1:T(8,128)}, f32[16,64]{0,1:T(8,128)S(1)}, u32[]{:S(2)}, u32[]{:S(2)}) collective-permute-start(f32[16,64]{0,1:T(8,128)} %bitcast.5), channel_id=1, source_target_pairs={{0,255},{1,0},{2,1},{3,2},{4,3},{5,4},{6,5},{7,6},{8,7},{9,8},{10,... | collective-permute-start | bytes 12296 | tf_op jit(solution)/shard_map/ppermute | solution.py:17
  16.4 61.4 %collective-permute-start.2 = (f32[16,64]{0,1:T(8,128)S(1)}, f32[16,64]{0,1:T(8,128)S(1)}, u32[]{:S(2)}, u32[]{:S(2)}) collective-permute-start(f32[16,64]{0,1:T(8,128)S(1)} %bitcast.346), channel_id=1, source_target_pairs={{0,4},{1,5},{2,6},{3,7},{4,8},{5,9},{6,10},{7,11},{8,12},{9,13},{1... | collective-permute-start | bytes 12296 | tf_op jit(solution)/shard_map/ppermute | solution.py:17
  19.8 58.5 %collective-permute-start.3 = (f32[16,64]{0,1:T(8,128)S(1)}, f32[16,64]{0,1:T(8,128)S(1)}, u32[]{:S(2)}, u32[]{:S(2)}) collective-permute-start(f32[16,64]{0,1:T(8,128)S(1)} %bitcast.345), channel_id=1, source_target_pairs={{0,252},{1,253},{2,254},{3,255},{4,0},{5,1},{6,2},{7,3},{8,4},{9,5... | collective-permute-start | bytes 12296 | tf_op jit(solution)/shard_map/ppermute | solution.py:17
  27.3 51.6 %collective-permute-start.4 = (f32[16,64]{0,1:T(8,128)S(1)}, f32[16,64]{0,1:T(8,128)S(1)}, u32[]{:S(2)}, u32[]{:S(2)}) collective-permute-start(f32[16,64]{0,1:T(8,128)S(1)} %bitcast.344), channel_id=1, source_target_pairs={{0,16},{1,17},{2,18},{3,19},{4,20},{5,21},{6,22},{7,23},{8,24},{9,... | collective-permute-start | bytes 12296 | tf_op jit(solution)/shard_map/ppermute | solution.py:17
  64.3 17.9 %collective-permute-start.5 = (f32[16,64]{0,1:T(8,128)}, f32[16,64]{0,1:T(8,128)S(1)}, u32[]{:S(2)}, u32[]{:S(2)}) collective-permute-start(f32[16,64]{0,1:T(8,128)} %bitcast.347), channel_id=1, source_target_pairs={{0,240},{1,241},{2,242},{3,243},{4,244},{5,245},{6,246},{7,247},{8... | collective-permute-start | bytes 12296 | tf_op jit(solution)/shard_map/ppermute | solution.py:17
  69.7 94.9 %collective-permute-start.12 = (f32[1,64]{1,0:T(1,128)}, f32[1,64]{1,0:T(1,128)}, u32[]{:S(2)}, u32[]{:S(2)}) collective-permute-start(f32[1,64]{1,0:T(1,128)} %get-tuple-element.87), channel_id=1, source_target_pairs={{0,255},{1,0},{2,1},{3,2},{4,3},{5,4},{6,5},{7,6},{8,7},{9,8},{10,... | collective-permute-start | bytes 776 | tf_op jit(solution)/shard_map/ppermute | solution.py:17
  77.7 87.3 %collective-permute-start.13 = (f32[1,64]{1,0:T(1,128)}, f32[1,64]{1,0:T(1,128)}, u32[]{:S(2)}, u32[]{:S(2)}) collective-permute-start(f32[1,64]{1,0:T(1,128)} %get-tuple-element.86), channel_id=1, source_target_pairs={{0,1},{1,2},{2,3},{3,4},{4,5},{5,6},{6,7},{7,8},{8,9},{9,10},{10,1... | collective-permute-start | bytes 776 | tf_op jit(solution)/shard_map/ppermute | solution.py:17
  78.4 87.7 %collective-permute-start.14 = (f32[1,64]{1,0:T(1,128)}, f32[1,64]{1,0:T(1,128)}, u32[]{:S(2)}, u32[]{:S(2)}) collective-permute-start(f32[1,64]{1,0:T(1,128)} %get-tuple-element.85), channel_id=1, source_target_pairs={{0,252},{1,253},{2,254},{3,255},{4,0},{5,1},{6,2},{7,3},{8,4},{9,5... | collective-permute-start | bytes 776 | tf_op jit(solution)/shard_map/ppermute | solution.py:17
  79.0 88.3 %collective-permute-start.15 = (f32[1,64]{1,0:T(1,128)}, f32[1,64]{1,0:T(1,128)}, u32[]{:S(2)}, u32[]{:S(2)}) collective-permute-start(f32[1,64]{1,0:T(1,128)} %get-tuple-element.84), channel_id=1, source_target_pairs={{0,4},{1,5},{2,6},{3,7},{4,8},{5,9},{6,10},{7,11},{8,12},{9,13},{1... | collective-permute-start | bytes 776 | tf_op jit(solution)/shard_map/ppermute | solution.py:17
  166.1 24.2 %collective-permute-start.7 = (f32[32,64]{0,1:T(8,128)S(1)}, f32[32,64]{0,1:T(8,128)S(1)}, u32[]{:S(2)}, u32[]{:S(2)}) collective-permute-start(f32[32,64]{0,1:T(8,128)S(1)} %get-tuple-element.59), channel_id=1, source_target_pairs={{0,1},{1,2},{2,3},{3,4},{4,5},{5,6},{6,7},{7,8},{8,9},{9,10},{10,1... | collective-permute-start | bytes 24584 | tf_op jit(solution)/shard_map/ppermute | solution.py:17
  167.3 25.9 %collective-permute-start.8 = (f32[32,64]{0,1:T(8,128)S(1)}, f32[32,64]{0,1:T(8,128)}, u32[]{:S(2)}, u32[]{:S(2)}) collective-permute-start(f32[32,64]{0,1:T(8,128)S(1)} %get-tuple-element.58), channel_id=1, source_target_pairs={{0,252},{1,253},{2,254},{3,255},{4,0},{5,1},{6,2},{7,3},{8,4},{9,5... | collective-permute-start | bytes 24584 | tf_op jit(solution)/shard_map/ppermute | solution.py:17
  176.1 20.2 %collective-permute-start.9 = (f32[32,64]{0,1:T(8,128)S(1)}, f32[32,64]{0,1:T(8,128)}, u32[]{:S(2)}, u32[]{:S(2)}) collective-permute-start(f32[32,64]{0,1:T(8,128)S(1)} %get-tuple-element.57), channel_id=1, source_target_pairs={{0,4},{1,5},{2,6},{3,7},{4,8},{5,9},{6,10},{7,11},{8,12},{9,13},{1... | collective-permute-start | bytes 24584 | tf_op jit(solution)/shard_map/ppermute | solution.py:17
  176.1 23.3 %collective-permute-start.10 = (f32[32,64]{0,1:T(8,128)S(1)}, f32[32,64]{0,1:T(8,128)}, u32[]{:S(2)}, u32[]{:S(2)}) collective-permute-start(f32[32,64]{0,1:T(8,128)S(1)} %get-tuple-element.56), channel_id=1, source_target_pairs={{0,240},{1,241},{2,242},{3,243},{4,244},{5,245},{6,246},{7,247},{8... | collective-permute-start | bytes 24584 | tf_op jit(solution)/shard_map/ppermute | solution.py:17
  176.6 25.9 %collective-permute-start.11 = (f32[32,64]{0,1:T(8,128)S(1)}, f32[32,64]{0,1:T(8,128)S(1)}, u32[]{:S(2)}, u32[]{:S(2)}) collective-permute-start(f32[32,64]{0,1:T(8,128)S(1)} %get-tuple-element.55), channel_id=1, source_target_pairs={{0,16},{1,17},{2,18},{3,19},{4,20},{5,21},{6,22},{7,23},{8,24},{9,... | collective-permute-start | bytes 24584 | tf_op jit(solution)/shard_map/ppermute | solution.py:17
  302.2 21.5 %collective-permute-start.18 = (f32[8,64]{0,1:T(8,128)S(1)}, f32[8,64]{0,1:T(8,128)S(1)}, u32[]{:S(2)}, u32[]{:S(2)}) collective-permute-start(f32[8,64]{0,1:T(8,128)S(1)} %bitcast.372), channel_id=1, source_target_pairs={{0,1},{1,2},{2,3},{3,4},{4,5},{5,6},{6,7},{7,8},{8,9},{9,10},{10,1... | collective-permute-start | bytes 6152 | tf_op jit(solution)/shard_map/ppermute | solution.py:17
  406.6 30.5 %collective-permute-start.25 = (f32[8,64]{0,1:T(8,128)}, f32[8,64]{0,1:T(8,128)}, u32[]{:S(2)}, u32[]{:S(2)}) collective-permute-start(f32[8,64]{0,1:T(8,128)} %get-tuple-element.53), channel_id=1, source_target_pairs={{0,1},{1,2},{2,3},{3,4},{4,5},{5,6},{6,7},{7,8},{8,9},{9,10},{10,1... | collective-permute-start | bytes 6152 | tf_op jit(solution)/shard_map/ppermute | solution.py:17
  406.6 33.6 %collective-permute-start.26 = (f32[8,64]{0,1:T(8,128)}, f32[8,64]{0,1:T(8,128)}, u32[]{:S(2)}, u32[]{:S(2)}) collective-permute-start(f32[8,64]{0,1:T(8,128)} %get-tuple-element.52), channel_id=1, source_target_pairs={{0,252},{1,253},{2,254},{3,255},{4,0},{5,1},{6,2},{7,3},{8,4},{9,5... | collective-permute-start | bytes 6152 | tf_op jit(solution)/shard_map/ppermute | solution.py:17
  409.5 33.7 %collective-permute-start.27 = (f32[8,64]{0,1:T(8,128)S(1)}, f32[8,64]{0,1:T(8,128)}, u32[]{:S(2)}, u32[]{:S(2)}) collective-permute-start(f32[8,64]{0,1:T(8,128)S(1)} %get-tuple-element.51), channel_id=1, source_target_pairs={{0,4},{1,5},{2,6},{3,7},{4,8},{5,9},{6,10},{7,11},{8,12},{9,13},{1... | collective-permute-start | bytes 6152 | tf_op jit(solution)/shard_map/ppermute | solution.py:17
  409.6 36.8 %collective-permute-start.28 = (f32[8,64]{0,1:T(8,128)S(1)}, f32[8,64]{0,1:T(8,128)}, u32[]{:S(2)}, u32[]{:S(2)}) collective-permute-start(f32[8,64]{0,1:T(8,128)S(1)} %get-tuple-element.50), channel_id=1, source_target_pairs={{0,240},{1,241},{2,242},{3,243},{4,244},{5,245},{6,246},{7,247},{8... | collective-permute-start | bytes 6152 | tf_op jit(solution)/shard_map/ppermute | solution.py:17
  413.0 36.5 %collective-permute-start.29 = (f32[8,64]{0,1:T(8,128)S(1)}, f32[8,64]{0,1:T(8,128)}, u32[]{:S(2)}, u32[]{:S(2)}) collective-permute-start(f32[8,64]{0,1:T(8,128)S(1)} %get-tuple-element.49), channel_id=1, source_target_pairs={{0,16},{1,17},{2,18},{3,19},{4,20},{5,21},{6,22},{7,23},{8,24},{9,... | collective-permute-start | bytes 6152 | tf_op jit(solution)/shard_map/ppermute | solution.py:17
  457.1 20.4 %collective-permute-start.30 = (f32[8,64]{0,1:T(8,128)S(1)}, f32[8,64]{0,1:T(8,128)S(1)}, u32[]{:S(2)}, u32[]{:S(2)}) collective-permute-start(f32[8,64]{0,1:T(8,128)S(1)} %bitcast.369), channel_id=1, source_target_pairs={{0,1},{1,2},{2,3},{3,4},{4,5},{5,6},{6,7},{7,8},{8,9},{9,10},{10,1... | collective-permute-start | bytes 6152 | tf_op jit(solution)/shard_map/ppermute | solution.py:17
  549.7 18.7 %collective-permute-start.36 = (f32[8,64]{0,1:T(8,128)S(1)}, f32[8,64]{0,1:T(8,128)S(1)}, u32[]{:S(2)}, u32[]{:S(2)}) collective-permute-start(f32[8,64]{0,1:T(8,128)S(1)} %get-tuple-element.48), channel_id=1, source_target_pairs={{0,255},{1,0},{2,1},{3,2},{4,3},{5,4},{6,5},{7,6},{8,7},{9,8},{10,... | collective-permute-start | bytes 6152 | tf_op jit(solution)/shard_map/ppermute | solution.py:17
  564.8 18.5 %collective-permute-start.40 = (f32[8,64]{0,1:T(8,128)S(1)}, f32[8,64]{0,1:T(8,128)S(1)}, u32[]{:S(2)}, u32[]{:S(2)}) collective-permute-start(f32[8,64]{0,1:T(8,128)S(1)} %get-tuple-element.44), channel_id=1, source_target_pairs={{0,240},{1,241},{2,242},{3,243},{4,244},{5,245},{6,246},{7,247},{8... | collective-permute-start | bytes 6152 | tf_op jit(solution)/shard_map/ppermute | solution.py:17
  569.0 17.2 %collective-permute-start.41 = (f32[8,64]{0,1:T(8,128)S(1)}, f32[8,64]{0,1:T(8,128)S(1)}, u32[]{:S(2)}, u32[]{:S(2)}) collective-permute-start(f32[8,64]{0,1:T(8,128)S(1)} %get-tuple-element.43), channel_id=1, source_target_pairs={{0,16},{1,17},{2,18},{3,19},{4,20},{5,21},{6,22},{7,23},{8,24},{9,... | collective-permute-start | bytes 6152 | tf_op jit(solution)/shard_map/ppermute | solution.py:17
  595.0 20.5 %collective-permute-start.42 = (f32[8,64]{0,1:T(8,128)}, f32[8,64]{0,1:T(8,128)S(1)}, u32[]{:S(2)}, u32[]{:S(2)}) collective-permute-start(f32[8,64]{0,1:T(8,128)} %bitcast.69), channel_id=1, source_target_pairs={{0,1},{1,2},{2,3},{3,4},{4,5},{5,6},{6,7},{7,8},{8,9},{9,10},{10,1... | collective-permute-start | bytes 6152 | tf_op jit(solution)/shard_map/ppermute | solution.py:17
  687.9 18.8 %collective-permute-start.48 = (f32[8,64]{0,1:T(8,128)S(1)}, f32[8,64]{0,1:T(8,128)S(1)}, u32[]{:S(2)}, u32[]{:S(2)}) collective-permute-start(f32[8,64]{0,1:T(8,128)S(1)} %get-tuple-element.42), channel_id=1, source_target_pairs={{0,255},{1,0},{2,1},{3,2},{4,3},{5,4},{6,5},{7,6},{8,7},{9,8},{10,... | collective-permute-start | bytes 6152 | tf_op jit(solution)/shard_map/ppermute | solution.py:17
  702.8 17.1 %collective-permute-start.51 = (f32[8,64]{0,1:T(8,128)S(1)}, f32[8,64]{0,1:T(8,128)S(1)}, u32[]{:S(2)}, u32[]{:S(2)}) collective-permute-start(f32[8,64]{0,1:T(8,128)S(1)} %get-tuple-element.39), channel_id=1, source_target_pairs={{0,4},{1,5},{2,6},{3,7},{4,8},{5,9},{6,10},{7,11},{8,12},{9,13},{1... | collective-permute-start | bytes 6152 | tf_op jit(solution)/shard_map/ppermute | solution.py:17
  702.8 28.8 %collective-permute-start.52 = (f32[8,64]{0,1:T(8,128)S(1)}, f32[8,64]{0,1:T(8,128)S(1)}, u32[]{:S(2)}, u32[]{:S(2)}) collective-permute-start(f32[8,64]{0,1:T(8,128)S(1)} %get-tuple-element.38), channel_id=1, source_target_pairs={{0,240},{1,241},{2,242},{3,243},{4,244},{5,245},{6,246},{7,247},{8... | collective-permute-start | bytes 6152 | tf_op jit(solution)/shard_map/ppermute | solution.py:17
  706.7 27.9 %collective-permute-start.53 = (f32[8,64]{0,1:T(8,128)S(1)}, f32[8,64]{0,1:T(8,128)S(1)}, u32[]{:S(2)}, u32[]{:S(2)}) collective-permute-start(f32[8,64]{0,1:T(8,128)S(1)} %get-tuple-element.37), channel_id=1, source_target_pairs={{0,16},{1,17},{2,18},{3,19},{4,20},{5,21},{6,22},{7,23},{8,24},{9,... | collective-permute-start | bytes 6152 | tf_op jit(solution)/shard_map/ppermute | solution.py:17
  712.1 51.0 %collective-permute-start.60 = (f32[1,32]{1,0:T(1,128)}, f32[1,32]{1,0:T(1,128)}, u32[]{:S(2)}, u32[]{:S(2)}) collective-permute-start(f32[1,32]{1,0:T(1,128)} %get-tuple-element.105), channel_id=1, source_target_pairs={{0,255},{1,0},{2,1},{3,2},{4,3},{5,4},{6,5},{7,6},{8,7},{9,8},{10,... | collective-permute-start | bytes 392 | tf_op jit(solution)/shard_map/ppermute | solution.py:17
  716.5 47.6 %collective-permute-start.61 = (f32[1,32]{1,0:T(1,128)}, f32[1,32]{1,0:T(1,128)}, u32[]{:S(2)}, u32[]{:S(2)}) collective-permute-start(f32[1,32]{1,0:T(1,128)} %get-tuple-element.104), channel_id=1, source_target_pairs={{0,1},{1,2},{2,3},{3,4},{4,5},{5,6},{6,7},{7,8},{8,9},{9,10},{10,1... | collective-permute-start | bytes 392 | tf_op jit(solution)/shard_map/ppermute | solution.py:17
  719.9 46.6 %collective-permute-start.62 = (f32[1,32]{1,0:T(1,128)}, f32[1,32]{1,0:T(1,128)}, u32[]{:S(2)}, u32[]{:S(2)}) collective-permute-start(f32[1,32]{1,0:T(1,128)} %get-tuple-element.103), channel_id=1, source_target_pairs={{0,252},{1,253},{2,254},{3,255},{4,0},{5,1},{6,2},{7,3},{8,4},{9,5... | collective-permute-start | bytes 392 | tf_op jit(solution)/shard_map/ppermute | solution.py:17
  731.6 34.9 %collective-permute-start.63 = (f32[1,32]{1,0:T(1,128)}, f32[1,32]{1,0:T(1,128)}, u32[]{:S(2)}, u32[]{:S(2)}) collective-permute-start(f32[1,32]{1,0:T(1,128)} %get-tuple-element.102), channel_id=1, source_target_pairs={{0,4},{1,5},{2,6},{3,7},{4,8},{5,9},{6,10},{7,11},{8,12},{9,13},{1... | collective-permute-start | bytes 392 | tf_op jit(solution)/shard_map/ppermute | solution.py:17
  757.1 20.3 %collective-permute-start.54 = (f32[8,32]{0,1:T(8,128)}, f32[8,32]{0,1:T(8,128)}, u32[]{:S(2)}, u32[]{:S(2)}) collective-permute-start(f32[8,32]{0,1:T(8,128)} %get-tuple-element.72), channel_id=1, source_target_pairs={{0,255},{1,0},{2,1},{3,2},{4,3},{5,4},{6,5},{7,6},{8,7},{9,8},{10,... | collective-permute-start | bytes 3080 | tf_op jit(solution)/shard_map/ppermute | solution.py:17
  766.5 19.3 %collective-permute-start.55 = (f32[8,32]{0,1:T(8,128)}, f32[8,32]{0,1:T(8,128)}, u32[]{:S(2)}, u32[]{:S(2)}) collective-permute-start(f32[8,32]{0,1:T(8,128)} %get-tuple-element.71), channel_id=1, source_target_pairs={{0,1},{1,2},{2,3},{3,4},{4,5},{5,6},{6,7},{7,8},{8,9},{9,10},{10,1... | collective-permute-start | bytes 3080 | tf_op jit(solution)/shard_map/ppermute | solution.py:17
  766.6 21.7 %collective-permute-start.56 = (f32[8,32]{0,1:T(8,128)S(1)}, f32[8,32]{0,1:T(8,128)}, u32[]{:S(2)}, u32[]{:S(2)}) collective-permute-start(f32[8,32]{0,1:T(8,128)S(1)} %get-tuple-element.70), channel_id=1, source_target_pairs={{0,252},{1,253},{2,254},{3,255},{4,0},{5,1},{6,2},{7,3},{8,4},{9,5... | collective-permute-start | bytes 3080 | tf_op jit(solution)/shard_map/ppermute | solution.py:17
  777.5 18.2 %collective-permute-start.59 = (f32[8,32]{0,1:T(8,128)S(1)}, f32[8,32]{0,1:T(8,128)}, u32[]{:S(2)}, u32[]{:S(2)}) collective-permute-start(f32[8,32]{0,1:T(8,128)S(1)} %get-tuple-element.67), channel_id=1, source_target_pairs={{0,16},{1,17},{2,18},{3,19},{4,20},{5,21},{6,22},{7,23},{8,24},{9,... | collective-permute-start | bytes 3080 | tf_op jit(solution)/shard_map/ppermute | solution.py:17
  802.1 32.9 %collective-permute-start.66 = (f32[8,32]{0,1:T(8,128)}, f32[8,32]{0,1:T(8,128)S(1)}, u32[]{:S(2)}, u32[]{:S(2)}) collective-permute-start(f32[8,32]{0,1:T(8,128)} %bitcast.112), channel_id=1, source_target_pairs={{0,1},{1,2},{2,3},{3,4},{4,5},{5,6},{6,7},{7,8},{8,9},{9,10},{10,1... | collective-permute-start | bytes 3080 | tf_op jit(solution)/shard_map/ppermute | solution.py:17
  815.2 25.1 %collective-permute-start.67 = (f32[8,32]{0,1:T(8,128)}, f32[8,32]{0,1:T(8,128)}, u32[]{:S(2)}, u32[]{:S(2)}) collective-permute-start(f32[8,32]{0,1:T(8,128)} %bitcast.113), channel_id=1, source_target_pairs={{0,255},{1,0},{2,1},{3,2},{4,3},{5,4},{6,5},{7,6},{8,7},{9,8},{10,... | collective-permute-start | bytes 3080 | tf_op jit(solution)/shard_map/ppermute | solution.py:17
  817.4 23.6 %collective-permute-start.68 = (f32[8,32]{0,1:T(8,128)}, f32[8,32]{0,1:T(8,128)S(1)}, u32[]{:S(2)}, u32[]{:S(2)}) collective-permute-start(f32[8,32]{0,1:T(8,128)} %bitcast.114), channel_id=1, source_target_pairs={{0,4},{1,5},{2,6},{3,7},{4,8},{5,9},{6,10},{7,11},{8,12},{9,13},{1... | collective-permute-start | bytes 3080 | tf_op jit(solution)/shard_map/ppermute | solution.py:17
  819.6 21.4 %collective-permute-start.69 = (f32[8,32]{0,1:T(8,128)}, f32[8,32]{0,1:T(8,128)S(1)}, u32[]{:S(2)}, u32[]{:S(2)}) collective-permute-start(f32[8,32]{0,1:T(8,128)} %bitcast.115), channel_id=1, source_target_pairs={{0,252},{1,253},{2,254},{3,255},{4,0},{5,1},{6,2},{7,3},{8,4},{9,5... | collective-permute-start | bytes 3080 | tf_op jit(solution)/shard_map/ppermute | solution.py:17
  874.8 19.3 %collective-permute-start.72 = (f32[8,32]{0,1:T(8,128)S(1)}, f32[8,32]{0,1:T(8,128)S(1)}, u32[]{:S(2)}, u32[]{:S(2)}) collective-permute-start(f32[8,32]{0,1:T(8,128)S(1)} %get-tuple-element.66), channel_id=1, source_target_pairs={{0,255},{1,0},{2,1},{3,2},{4,3},{5,4},{6,5},{7,6},{8,7},{9,8},{10,... | collective-permute-start | bytes 3080 | tf_op jit(solution)/shard_map/ppermute | solution.py:17
  888.8 16.5 %collective-permute-start.76 = (f32[8,32]{0,1:T(8,128)S(1)}, f32[8,32]{0,1:T(8,128)}, u32[]{:S(2)}, u32[]{:S(2)}) collective-permute-start(f32[8,32]{0,1:T(8,128)S(1)} %get-tuple-element.62), channel_id=1, source_target_pairs={{0,240},{1,241},{2,242},{3,243},{4,244},{5,245},{6,246},{7,247},{8... | collective-permute-start | bytes 3080 | tf_op jit(solution)/shard_map/ppermute | solution.py:17
  914.5 20.7 %collective-permute-start.78 = (f32[8,32]{0,1:T(8,128)}, f32[8,32]{0,1:T(8,128)}, u32[]{:S(2)}, u32[]{:S(2)}) collective-permute-start(f32[8,32]{0,1:T(8,128)} %bitcast.128), channel_id=1, source_target_pairs={{0,1},{1,2},{2,3},{3,4},{4,5},{5,6},{6,7},{7,8},{8,9},{9,10},{10,1... | collective-permute-start | bytes 3080 | tf_op jit(solution)/shard_map/ppermute | solution.py:17
  953.8 33.9 %collective-permute-start.84 = (f32[8,64]{0,1:T(8,128)S(1)}, f32[8,64]{0,1:T(8,128)S(1)}, u32[]{:S(2)}, u32[]{:S(2)}) collective-permute-start(f32[8,64]{0,1:T(8,128)S(1)} %bitcast.371), channel_id=1, source_target_pairs={{0,1},{1,2},{2,3},{3,4},{4,5},{5,6},{6,7},{7,8},{8,9},{9,10},{10,1... | collective-permute-start | bytes 6152 | tf_op jit(solution)/shard_map/ppermute | solution.py:17
  972.9 20.4 %collective-permute-start.85 = (f32[8,64]{0,1:T(8,128)}, f32[8,64]{0,1:T(8,128)S(1)}, u32[]{:S(2)}, u32[]{:S(2)}) collective-permute-start(f32[8,64]{0,1:T(8,128)} %bitcast.139), channel_id=1, source_target_pairs={{0,255},{1,0},{2,1},{3,2},{4,3},{5,4},{6,5},{7,6},{8,7},{9,8},{10,... | collective-permute-start | bytes 6152 | tf_op jit(solution)/shard_map/ppermute | solution.py:17
  (106 other events, 5222.0 us)
Sparse Core Ops, SparseCore 0:
  1092.0 118.6 all-gather.2
